TPU v7x, 32 devices: a whole 2x2x4 slice. The times are simulated.
32 devices in a mesh: var: 16 (over z, x, core), smp: 2 (over y).
Axes of the slice: x: 2, y: 2, z: 4, core: 2. Of those that a mesh axis runs over, the one named last changes fastest.
Arguments:
- genotypes: bfloat16 [1024, 8192], P('smp', 'var'), may hold values from -4 to 4, as said below
- marginal: float32 [8192, 256], P('var', 'smp'), may hold values from -6 to 6
- block_inverse: float32 [32, 256, 256], P('var'), may hold values from -1 to 1, as said below
Outputs:
- weights: float32 [8192, 256], P('var', 'smp')
Inputs may be any that keep to these rules, and one draw needn't show every extreme that they name: `genotypes`: each variant's column has mean about 0 and variance about 1 over the samples. `block_inverse`: matrices near the identity divided by 1.5, with independent entrywise jitter; they are not derived from R.
All inputs are finite; a program needn't handle non-finite values.
Results may differ from a plain program's by a relative error of at most 0.0003.
Values may be sent and summed in bfloat16 or wider, within the bound.
A program may use at most 64 MiB of HBM per device.

v0:
```python
import jax
import jax.numpy as jnp
from jax import lax
from jax.sharding import PartitionSpec as P

SWEEPS = 2


ridge_weight = 0.5


def passed_along(value, axis, steps):
    count = lax.axis_size(axis)
    leading, last = (max(0, -steps), min(count, count - steps))
    return lax.ppermute(value, axis, [(source, source + steps) for source in range(leading, last)])


def gram_blocks(own_samples, rim_samples, group):
    sample_count, variant_count = own_samples.shape
    groups_dev = variant_count // group
    extended = jnp.concatenate([own_samples, rim_samples], 1)
    own_cols = own_samples.reshape(sample_count, groups_dev, group)
    results = []
    for offset in range(3):
        partner = extended[:, offset * group : offset * group + variant_count].reshape(
            sample_count, groups_dev, group
        )
        product = jnp.einsum("snc,snd->ncd", own_cols, partner, preferred_element_type=jnp.float32)
        if offset == 2:
            product = jnp.tril(product)
        results.append(product)
    return jnp.stack(results, 1)


def slab_sweep(linkage, inverse, weights, target, upstream):
    group = inverse.shape[1]
    band = 2 * group
    count = inverse.shape[0]
    rows = weights.shape[0]
    cols = weights.shape[1]
    padded = jnp.concatenate([jnp.zeros((band, cols), jnp.float32), weights, upstream], 0)
    lowered = jnp.concatenate([jnp.zeros((2, 3, group, group), jnp.float32), linkage], 0)
    highest = lax.Precision.HIGHEST

    def slab_advance(group_index, state):
        base = band + group_index * group
        current = lax.dynamic_slice_in_dim(state, base, group, 0)
        remain = (
            lax.dynamic_slice_in_dim(target, group_index * group, group, 0) - ridge_weight * current
        )
        for offset in range(3):
            remain = remain - jnp.dot(
                linkage[group_index, offset],
                lax.dynamic_slice_in_dim(state, base + offset * group, group, 0),
                precision=highest,
            )
        for offset in (1, 2):
            remain = remain - jnp.dot(
                lowered[group_index + 2 - offset, offset].T,
                lax.dynamic_slice_in_dim(state, base - offset * group, group, 0),
                precision=highest,
            )
        updated = current + jnp.dot(inverse[group_index], remain, precision=highest)
        return lax.dynamic_update_slice_in_dim(state, updated, base, 0)

    padded = lax.fori_loop(0, count, slab_advance, padded)
    weights = padded[band : band + rows]
    last_rows = weights[(count - 1) * group :]
    before_rows = weights[(count - 2) * group : (count - 1) * group]
    first_part = jnp.dot(linkage[count - 1, 1].T, last_rows, precision=highest) + jnp.dot(
        linkage[count - 2, 2].T, before_rows, precision=highest
    )
    second_part = jnp.dot(linkage[count - 1, 2].T, last_rows, precision=highest)
    return (weights, jnp.concatenate([first_part, second_part], 0))


def per_device(genotypes, marginal, block_inverse):
    group = block_inverse.shape[1]
    band = 2 * group
    variant_count = genotypes.shape[1]
    trait_count = marginal.shape[1]
    rim_cols = passed_along(genotypes, "var", -1)
    sample_total = genotypes.shape[0] * lax.axis_size("smp")
    linkage = lax.psum(gram_blocks(genotypes, rim_cols, group), "smp") / sample_total
    position = lax.axis_index("var")
    var_count = lax.axis_size("var")
    rest_zeros = jnp.zeros((variant_count - band, trait_count), jnp.float32)
    band_zeros = jnp.zeros((band, trait_count), jnp.float32)
    weights = jnp.zeros((variant_count, trait_count), jnp.float32)

    def hold(held):
        return (held, band_zeros)

    upstream = band_zeros
    for sweep_index in range(SWEEPS):
        if sweep_index > 0:
            upstream = passed_along(weights, "var", -1)

        def turn(turn_index, state_pair):
            current, inflow = state_pair

            def turn_advance(held):
                target = marginal - jnp.concatenate([inflow, rest_zeros], 0)
                return slab_sweep(linkage, block_inverse, held, target, upstream)

            current, outflow = lax.cond(turn_index == position, turn_advance, hold, current)
            received = passed_along(outflow, "var", 1)
            return (current, received)

        weights, leftover = lax.fori_loop(0, var_count, turn, (weights, band_zeros))
    return weights


def solution(mesh):
    return jax.shard_map(
        per_device,
        mesh=mesh,
        in_specs=(P("smp", "var"), P("var", "smp"), P("var", None, None)),
        out_specs=P("var", "smp"),
        check_vma=False,
    )
```

profile of v0, /device:TPU:26, one launch (start us, length us, event | category | flops | bytes accessed | tf_op | source)
XLA Modules:
  0.0 687.4 jit_solution(4183110730919878862)
XLA Ops:
  18.4 53.8 %all-reduce.4.cloned.1.call-done = f32[2,3,256,256]{3,2,0,1:T(8,128)} async-done(((f32[2,3,256,256]{3,2,0,1:T(8,128)}), f32[2,3,256,256]{3,2,0,1:T(8,128)}) %all-reduce.4.cloned.1.call-update) | async-done | bytes 1572880 | tf_op jit(solution)/shard_map/psum | solution.py:84
  74.9 338.4 %while.70 = (s32[]{:T(128)}, f32[512,128]{1,0:T(8,128)S(1)}, f32[512,128]{0,1:T(8,128)}, s32[]{:T(128)}, f32[512,128]{1,0:T(8,128)}, /*index=5*/f32[2,3,256,256]...) while((s32[]{:T(128)}, f32[512,128]{1,0:T(8,128)S(1)}, f32[512,128]{0,1:T(8,128)}, s32[]{:T(128)}, ...), condition=%wide.region_6.7_spmd, body=%wide.region_1.6_spmd.sunk | while | flops 906788864 | bytes 16517993 | solution.py:110
  77.5 6.0 collective-permute-done.1
  86.8 6.0 collective-permute-done.1
  96.1 6.0 collective-permute-done.1
  105.4 6.0 collective-permute-done.1
  114.7 6.0 collective-permute-done.1
  152.0 6.4 collective-permute-done.1
  161.8 6.9 collective-permute-done.1
  172.0 6.9 collective-permute-done.1
  182.2 6.9 collective-permute-done.1
  192.4 6.9 collective-permute-done.1
  202.6 170.6 %collective-permute-done.1 = f32[512,128]{0,1:T(8,128)S(1)} collective-permute-done((f32[512,128]{0,1:T(8,128)}, f32[512,128]{0,1:T(8,128)S(1)}, u32[]{:S(2)}, u32[]{:S(2)}) %collective-permute-start.1) | collective-permute-done | bytes 262176 | tf_op jit(solution)/shard_map/while/body/eval_jaxpr/ppermute | solution.py:15
  373.9 15.5 %conditional.4 = (f32[512,128]{1,0:T(8,128)S(1)}, f32[512,128]{0,1:T(8,128)}) conditional(s32[]{:T(128)} %convert_element_type.16, f32[512,128]{1,0:T(8,128)S(1)} %get-tuple-element.1152, (f32[512,128]{1,0:T(8,128)S(1)}, f32[512,128]{1,0:T(8,128)}, f32[512,128]{0,1:T(8,128)}, f32[2,3,256,256]{3,2,1,0:T(8,128)S(1)}, ...), branch_computations={%region_2.2_spmd, %region_3.5_spmd} | conditional | flops 906788864 | bytes 14420634 | solution.py:106
  378.0 9.5 %while.68 = (s32[]{:T(128)}, f32[1536,128]{1,0:T(8,128)S(1)}, f32[2,256,256]{2,1,0:T(8,128)S(1)}, f32[512,128]{1,0:T(8,128)S(1)}, f32[2,3,256,256]{3,2,1,0:T(8,1...) while((s32[]{:T(128)}, f32[1536,128]{1,0:T(8,128)S(1)}, ...), condition=%wide.region_5.4_spmd, body=%wide.region_4.3_spmd.sunk | while | flops 604241920 | bytes 4065770 | solution.py:66
  391.4 6.0 collective-permute-done.1
  398.8 12.5 %collective-permute-start.1 = (f32[512,128]{0,1:T(8,128)}, f32[512,128]{0,1:T(8,128)S(1)}, u32[]{:S(2)}, u32[]{:S(2)}) collective-permute-start(f32[512,128]{0,1:T(8,128)} %get-tuple-element.1004), channel_id=1, source_target_pairs={{0,2},{2,4},{4,6},{6,8},{8,10},{10,12},{12,14},{14,16},{16,18},{18... | collective-permute-start | bytes 786440 | tf_op jit(solution)/shard_map/while/body/eval_jaxpr/ppermute | solution.py:15
  421.5 258.4 %while.71 = (s32[]{:T(128)}, f32[512,128]{1,0:T(8,128)S(1)}, f32[512,128]{0,1:T(8,128)}, s32[]{:T(128)}, f32[512,128]{1,0:T(8,128)}, /*index=5*/f32[512,128]{1,0...) while((s32[]{:T(128)}, f32[512,128]{1,0:T(8,128)S(1)}, ...), condition=%wide.region_12.13_spmd, body=%wide.region_7.12_spmd.sunk | while | flops 906788864 | bytes 16272253 | solution.py:110
  424.1 6.2 collective-permute-done
  470.9 6.0 collective-permute-done
  480.3 6.0 collective-permute-done
  489.6 6.0 collective-permute-done
  498.9 6.0 collective-permute-done
  508.2 6.0 collective-permute-done
  517.5 6.0 collective-permute-done
  526.8 6.0 collective-permute-done
  536.1 6.1 collective-permute-done
  545.5 91.9 %collective-permute-done = f32[512,128]{0,1:T(8,128)S(1)} collective-permute-done((f32[512,128]{0,1:T(8,128)}, f32[512,128]{0,1:T(8,128)S(1)}, u32[]{:S(2)}, u32[]{:S(2)}) %collective-permute-start) | collective-permute-done | bytes 262176 | tf_op jit(solution)/shard_map/while/body/eval_jaxpr/ppermute | solution.py:15
  638.2 16.7 %conditional.5 = (f32[512,128]{1,0:T(8,128)S(1)}, f32[512,128]{0,1:T(8,128)}) conditional(s32[]{:T(128)} %convert_element_type.17, f32[512,128]{1,0:T(8,128)S(1)} %get-tuple-element.1177, (f32[512,128]{1,0:T(8,128)S(1)}, f32[512,128]{1,0:T(8,128)}, f32[512,128]{1,0:T(8,128)}, f32[512,128]{0,1:T(8,128)}, f32[2,3,256,256]{3,2,1,0:T(8,128)S(1)}, ...), branch_computations={%region_8.8_spmd, %region_9.11_spmd} | conditional | flops 906788864 | bytes 14174878 | solution.py:106
  643.4 9.5 %while.69 = (s32[]{:T(128)}, f32[1536,128]{1,0:T(8,128)S(1)}, f32[2,256,256]{2,1,0:T(8,128)S(1)}, f32[512,128]{1,0:T(8,128)S(1)}, f32[2,3,256,256]{3,2,1,0:T(8,1...) while((s32[]{:T(128)}, f32[1536,128]{1,0:T(8,128)S(1)}, ...), condition=%wide.region_11.10_spmd, body=%wide.region_10.9_spmd.sunk | while | flops 604241920 | bytes 4065770 | solution.py:66
  656.8 6.0 collective-permute-done
  664.2 13.6 %collective-permute-start = (f32[512,128]{0,1:T(8,128)}, f32[512,128]{0,1:T(8,128)S(1)}, u32[]{:S(2)}, u32[]{:S(2)}) collective-permute-start(f32[512,128]{0,1:T(8,128)} %get-tuple-element.1014), channel_id=1, source_target_pairs={{0,2},{2,4},{4,6},{6,8},{8,10},{10,12},{12,14},{14,16},{16,18},{18... | collective-permute-start | bytes 786440 | tf_op jit(solution)/shard_map/while/body/eval_jaxpr/ppermute | solution.py:15
  (232 shorter events, 222.2 us)
Async XLA Ops:
  6.5 65.7 %all-reduce.4.cloned.1.call-start = ((), (), s32[]{:S(2)}) async-start(), calls=%async_computation | async-start | bytes 3145728 | tf_op jit(solution)/shard_map/psum | solution.py:84
  7.8 8.6 %collective-permute-start.2 = (bf16[512,512]{0,1:T(8,128)(2,1)S(1)}, bf16[512,512]{0,1:T(8,128)(2,1)S(1)}, u32[]{:S(2)}, u32[]{:S(2)}) collective-permute-start(bf16[512,512]{0,1:T(8,128)(2,1)S(1)} %copy.39), channel_id=1, source_target_pairs={{2,0},{4,2},{6,4},{8,6},{10,8},{12,10},{14,12},{16,14},{18,16},{20... | collective-permute-start | bytes 1572872 | tf_op jit(solution)/shard_map/ppermute | solution.py:15
  75.6 7.9 %collective-permute-start.1 = (f32[512,128]{0,1:T(8,128)}, f32[512,128]{0,1:T(8,128)S(1)}, u32[]{:S(2)}, u32[]{:S(2)}) collective-permute-start(f32[512,128]{0,1:T(8,128)} %get-tuple-element.1004), channel_id=1, source_target_pairs={{0,2},{2,4},{4,6},{6,8},{8,10},{10,12},{12,14},{14,16},{16,18},{18... | collective-permute-start | bytes 786440 | tf_op jit(solution)/shard_map/while/body/eval_jaxpr/ppermute | solution.py:15
  84.9 7.9 %collective-permute-start.1 = (f32[512,128]{0,1:T(8,128)}, f32[512,128]{0,1:T(8,128)S(1)}, u32[]{:S(2)}, u32[]{:S(2)}) collective-permute-start(f32[512,128]{0,1:T(8,128)} %get-tuple-element.1004), channel_id=1, source_target_pairs={{0,2},{2,4},{4,6},{6,8},{8,10},{10,12},{12,14},{14,16},{16,18},{18... | collective-permute-start | bytes 786440 | tf_op jit(solution)/shard_map/while/body/eval_jaxpr/ppermute | solution.py:15
  94.2 7.9 %collective-permute-start.1 = (f32[512,128]{0,1:T(8,128)}, f32[512,128]{0,1:T(8,128)S(1)}, u32[]{:S(2)}, u32[]{:S(2)}) collective-permute-start(f32[512,128]{0,1:T(8,128)} %get-tuple-element.1004), channel_id=1, source_target_pairs={{0,2},{2,4},{4,6},{6,8},{8,10},{10,12},{12,14},{14,16},{16,18},{18... | collective-permute-start | bytes 786440 | tf_op jit(solution)/shard_map/while/body/eval_jaxpr/ppermute | solution.py:15
  103.5 7.9 %collective-permute-start.1 = (f32[512,128]{0,1:T(8,128)}, f32[512,128]{0,1:T(8,128)S(1)}, u32[]{:S(2)}, u32[]{:S(2)}) collective-permute-start(f32[512,128]{0,1:T(8,128)} %get-tuple-element.1004), channel_id=1, source_target_pairs={{0,2},{2,4},{4,6},{6,8},{8,10},{10,12},{12,14},{14,16},{16,18},{18... | collective-permute-start | bytes 786440 | tf_op jit(solution)/shard_map/while/body/eval_jaxpr/ppermute | solution.py:15
  112.8 7.9 %collective-permute-start.1 = (f32[512,128]{0,1:T(8,128)}, f32[512,128]{0,1:T(8,128)S(1)}, u32[]{:S(2)}, u32[]{:S(2)}) collective-permute-start(f32[512,128]{0,1:T(8,128)} %get-tuple-element.1004), channel_id=1, source_target_pairs={{0,2},{2,4},{4,6},{6,8},{8,10},{10,12},{12,14},{14,16},{16,18},{18... | collective-permute-start | bytes 786440 | tf_op jit(solution)/shard_map/while/body/eval_jaxpr/ppermute | solution.py:15
  122.1 7.9 %collective-permute-start.1 = (f32[512,128]{0,1:T(8,128)}, f32[512,128]{0,1:T(8,128)S(1)}, u32[]{:S(2)}, u32[]{:S(2)}) collective-permute-start(f32[512,128]{0,1:T(8,128)} %get-tuple-element.1004), channel_id=1, source_target_pairs={{0,2},{2,4},{4,6},{6,8},{8,10},{10,12},{12,14},{14,16},{16,18},{18... | collective-permute-start | bytes 786440 | tf_op jit(solution)/shard_map/while/body/eval_jaxpr/ppermute | solution.py:15
  131.4 7.9 %collective-permute-start.1 = (f32[512,128]{0,1:T(8,128)}, f32[512,128]{0,1:T(8,128)S(1)}, u32[]{:S(2)}, u32[]{:S(2)}) collective-permute-start(f32[512,128]{0,1:T(8,128)} %get-tuple-element.1004), channel_id=1, source_target_pairs={{0,2},{2,4},{4,6},{6,8},{8,10},{10,12},{12,14},{14,16},{16,18},{18... | collective-permute-start | bytes 786440 | tf_op jit(solution)/shard_map/while/body/eval_jaxpr/ppermute | solution.py:15
  140.8 7.9 %collective-permute-start.1 = (f32[512,128]{0,1:T(8,128)}, f32[512,128]{0,1:T(8,128)S(1)}, u32[]{:S(2)}, u32[]{:S(2)}) collective-permute-start(f32[512,128]{0,1:T(8,128)} %get-tuple-element.1004), channel_id=1, source_target_pairs={{0,2},{2,4},{4,6},{6,8},{8,10},{10,12},{12,14},{14,16},{16,18},{18... | collective-permute-start | bytes 786440 | tf_op jit(solution)/shard_map/while/body/eval_jaxpr/ppermute | solution.py:15
  150.1 8.4 %collective-permute-start.1 = (f32[512,128]{0,1:T(8,128)}, f32[512,128]{0,1:T(8,128)S(1)}, u32[]{:S(2)}, u32[]{:S(2)}) collective-permute-start(f32[512,128]{0,1:T(8,128)} %get-tuple-element.1004), channel_id=1, source_target_pairs={{0,2},{2,4},{4,6},{6,8},{8,10},{10,12},{12,14},{14,16},{16,18},{18... | collective-permute-start | bytes 786440 | tf_op jit(solution)/shard_map/while/body/eval_jaxpr/ppermute | solution.py:15
  159.9 8.8 %collective-permute-start.1 = (f32[512,128]{0,1:T(8,128)}, f32[512,128]{0,1:T(8,128)S(1)}, u32[]{:S(2)}, u32[]{:S(2)}) collective-permute-start(f32[512,128]{0,1:T(8,128)} %get-tuple-element.1004), channel_id=1, source_target_pairs={{0,2},{2,4},{4,6},{6,8},{8,10},{10,12},{12,14},{14,16},{16,18},{18... | collective-permute-start | bytes 786440 | tf_op jit(solution)/shard_map/while/body/eval_jaxpr/ppermute | solution.py:15
  170.1 8.8 %collective-permute-start.1 = (f32[512,128]{0,1:T(8,128)}, f32[512,128]{0,1:T(8,128)S(1)}, u32[]{:S(2)}, u32[]{:S(2)}) collective-permute-start(f32[512,128]{0,1:T(8,128)} %get-tuple-element.1004), channel_id=1, source_target_pairs={{0,2},{2,4},{4,6},{6,8},{8,10},{10,12},{12,14},{14,16},{16,18},{18... | collective-permute-start | bytes 786440 | tf_op jit(solution)/shard_map/while/body/eval_jaxpr/ppermute | solution.py:15
  180.3 8.8 %collective-permute-start.1 = (f32[512,128]{0,1:T(8,128)}, f32[512,128]{0,1:T(8,128)S(1)}, u32[]{:S(2)}, u32[]{:S(2)}) collective-permute-start(f32[512,128]{0,1:T(8,128)} %get-tuple-element.1004), channel_id=1, source_target_pairs={{0,2},{2,4},{4,6},{6,8},{8,10},{10,12},{12,14},{14,16},{16,18},{18... | collective-permute-start | bytes 786440 | tf_op jit(solution)/shard_map/while/body/eval_jaxpr/ppermute | solution.py:15
  190.5 8.8 %collective-permute-start.1 = (f32[512,128]{0,1:T(8,128)}, f32[512,128]{0,1:T(8,128)S(1)}, u32[]{:S(2)}, u32[]{:S(2)}) collective-permute-start(f32[512,128]{0,1:T(8,128)} %get-tuple-element.1004), channel_id=1, source_target_pairs={{0,2},{2,4},{4,6},{6,8},{8,10},{10,12},{12,14},{14,16},{16,18},{18... | collective-permute-start | bytes 786440 | tf_op jit(solution)/shard_map/while/body/eval_jaxpr/ppermute | solution.py:15
  200.7 172.5 %collective-permute-start.1 = (f32[512,128]{0,1:T(8,128)}, f32[512,128]{0,1:T(8,128)S(1)}, u32[]{:S(2)}, u32[]{:S(2)}) collective-permute-start(f32[512,128]{0,1:T(8,128)} %get-tuple-element.1004), channel_id=1, source_target_pairs={{0,2},{2,4},{4,6},{6,8},{8,10},{10,12},{12,14},{14,16},{16,18},{18... | collective-permute-start | bytes 786440 | tf_op jit(solution)/shard_map/while/body/eval_jaxpr/ppermute | solution.py:15
  389.4 7.9 %collective-permute-start.1 = (f32[512,128]{0,1:T(8,128)}, f32[512,128]{0,1:T(8,128)S(1)}, u32[]{:S(2)}, u32[]{:S(2)}) collective-permute-start(f32[512,128]{0,1:T(8,128)} %get-tuple-element.1004), channel_id=1, source_target_pairs={{0,2},{2,4},{4,6},{6,8},{8,10},{10,12},{12,14},{14,16},{16,18},{18... | collective-permute-start | bytes 786440 | tf_op jit(solution)/shard_map/while/body/eval_jaxpr/ppermute | solution.py:15
  398.8 13.8 %collective-permute-start.1 = (f32[512,128]{0,1:T(8,128)}, f32[512,128]{0,1:T(8,128)S(1)}, u32[]{:S(2)}, u32[]{:S(2)}) collective-permute-start(f32[512,128]{0,1:T(8,128)} %get-tuple-element.1004), channel_id=1, source_target_pairs={{0,2},{2,4},{4,6},{6,8},{8,10},{10,12},{12,14},{14,16},{16,18},{18... | collective-permute-start | bytes 786440 | tf_op jit(solution)/shard_map/while/body/eval_jaxpr/ppermute | solution.py:15
  422.2 8.2 %collective-permute-start = (f32[512,128]{0,1:T(8,128)}, f32[512,128]{0,1:T(8,128)S(1)}, u32[]{:S(2)}, u32[]{:S(2)}) collective-permute-start(f32[512,128]{0,1:T(8,128)} %get-tuple-element.1014), channel_id=1, source_target_pairs={{0,2},{2,4},{4,6},{6,8},{8,10},{10,12},{12,14},{14,16},{16,18},{18... | collective-permute-start | bytes 786440 | tf_op jit(solution)/shard_map/while/body/eval_jaxpr/ppermute | solution.py:15
  431.8 7.9 %collective-permute-start = (f32[512,128]{0,1:T(8,128)}, f32[512,128]{0,1:T(8,128)S(1)}, u32[]{:S(2)}, u32[]{:S(2)}) collective-permute-start(f32[512,128]{0,1:T(8,128)} %get-tuple-element.1014), channel_id=1, source_target_pairs={{0,2},{2,4},{4,6},{6,8},{8,10},{10,12},{12,14},{14,16},{16,18},{18... | collective-permute-start | bytes 786440 | tf_op jit(solution)/shard_map/while/body/eval_jaxpr/ppermute | solution.py:15
  441.1 7.9 %collective-permute-start = (f32[512,128]{0,1:T(8,128)}, f32[512,128]{0,1:T(8,128)S(1)}, u32[]{:S(2)}, u32[]{:S(2)}) collective-permute-start(f32[512,128]{0,1:T(8,128)} %get-tuple-element.1014), channel_id=1, source_target_pairs={{0,2},{2,4},{4,6},{6,8},{8,10},{10,12},{12,14},{14,16},{16,18},{18... | collective-permute-start | bytes 786440 | tf_op jit(solution)/shard_map/while/body/eval_jaxpr/ppermute | solution.py:15
  450.4 7.9 %collective-permute-start = (f32[512,128]{0,1:T(8,128)}, f32[512,128]{0,1:T(8,128)S(1)}, u32[]{:S(2)}, u32[]{:S(2)}) collective-permute-start(f32[512,128]{0,1:T(8,128)} %get-tuple-element.1014), channel_id=1, source_target_pairs={{0,2},{2,4},{4,6},{6,8},{8,10},{10,12},{12,14},{14,16},{16,18},{18... | collective-permute-start | bytes 786440 | tf_op jit(solution)/shard_map/while/body/eval_jaxpr/ppermute | solution.py:15
  459.7 7.9 %collective-permute-start = (f32[512,128]{0,1:T(8,128)}, f32[512,128]{0,1:T(8,128)S(1)}, u32[]{:S(2)}, u32[]{:S(2)}) collective-permute-start(f32[512,128]{0,1:T(8,128)} %get-tuple-element.1014), channel_id=1, source_target_pairs={{0,2},{2,4},{4,6},{6,8},{8,10},{10,12},{12,14},{14,16},{16,18},{18... | collective-permute-start | bytes 786440 | tf_op jit(solution)/shard_map/while/body/eval_jaxpr/ppermute | solution.py:15
  469.0 7.9 %collective-permute-start = (f32[512,128]{0,1:T(8,128)}, f32[512,128]{0,1:T(8,128)S(1)}, u32[]{:S(2)}, u32[]{:S(2)}) collective-permute-start(f32[512,128]{0,1:T(8,128)} %get-tuple-element.1014), channel_id=1, source_target_pairs={{0,2},{2,4},{4,6},{6,8},{8,10},{10,12},{12,14},{14,16},{16,18},{18... | collective-permute-start | bytes 786440 | tf_op jit(solution)/shard_map/while/body/eval_jaxpr/ppermute | solution.py:15
  478.3 7.9 %collective-permute-start = (f32[512,128]{0,1:T(8,128)}, f32[512,128]{0,1:T(8,128)S(1)}, u32[]{:S(2)}, u32[]{:S(2)}) collective-permute-start(f32[512,128]{0,1:T(8,128)} %get-tuple-element.1014), channel_id=1, source_target_pairs={{0,2},{2,4},{4,6},{6,8},{8,10},{10,12},{12,14},{14,16},{16,18},{18... | collective-permute-start | bytes 786440 | tf_op jit(solution)/shard_map/while/body/eval_jaxpr/ppermute | solution.py:15
  487.6 7.9 %collective-permute-start = (f32[512,128]{0,1:T(8,128)}, f32[512,128]{0,1:T(8,128)S(1)}, u32[]{:S(2)}, u32[]{:S(2)}) collective-permute-start(f32[512,128]{0,1:T(8,128)} %get-tuple-element.1014), channel_id=1, source_target_pairs={{0,2},{2,4},{4,6},{6,8},{8,10},{10,12},{12,14},{14,16},{16,18},{18... | collective-permute-start | bytes 786440 | tf_op jit(solution)/shard_map/while/body/eval_jaxpr/ppermute | solution.py:15
  497.0 7.9 %collective-permute-start = (f32[512,128]{0,1:T(8,128)}, f32[512,128]{0,1:T(8,128)S(1)}, u32[]{:S(2)}, u32[]{:S(2)}) collective-permute-start(f32[512,128]{0,1:T(8,128)} %get-tuple-element.1014), channel_id=1, source_target_pairs={{0,2},{2,4},{4,6},{6,8},{8,10},{10,12},{12,14},{14,16},{16,18},{18... | collective-permute-start | bytes 786440 | tf_op jit(solution)/shard_map/while/body/eval_jaxpr/ppermute | solution.py:15
  524.9 7.9 %collective-permute-start = (f32[512,128]{0,1:T(8,128)}, f32[512,128]{0,1:T(8,128)S(1)}, u32[]{:S(2)}, u32[]{:S(2)}) collective-permute-start(f32[512,128]{0,1:T(8,128)} %get-tuple-element.1014), channel_id=1, source_target_pairs={{0,2},{2,4},{4,6},{6,8},{8,10},{10,12},{12,14},{14,16},{16,18},{18... | collective-permute-start | bytes 786440 | tf_op jit(solution)/shard_map/while/body/eval_jaxpr/ppermute | solution.py:15
  534.2 8.0 %collective-permute-start = (f32[512,128]{0,1:T(8,128)}, f32[512,128]{0,1:T(8,128)S(1)}, u32[]{:S(2)}, u32[]{:S(2)}) collective-permute-start(f32[512,128]{0,1:T(8,128)} %get-tuple-element.1014), channel_id=1, source_target_pairs={{0,2},{2,4},{4,6},{6,8},{8,10},{10,12},{12,14},{14,16},{16,18},{18... | collective-permute-start | bytes 786440 | tf_op jit(solution)/shard_map/while/body/eval_jaxpr/ppermute | solution.py:15
  543.6 93.9 %collective-permute-start = (f32[512,128]{0,1:T(8,128)}, f32[512,128]{0,1:T(8,128)S(1)}, u32[]{:S(2)}, u32[]{:S(2)}) collective-permute-start(f32[512,128]{0,1:T(8,128)} %get-tuple-element.1014), channel_id=1, source_target_pairs={{0,2},{2,4},{4,6},{6,8},{8,10},{10,12},{12,14},{14,16},{16,18},{18... | collective-permute-start | bytes 786440 | tf_op jit(solution)/shard_map/while/body/eval_jaxpr/ppermute | solution.py:15
  654.9 7.9 %collective-permute-start = (f32[512,128]{0,1:T(8,128)}, f32[512,128]{0,1:T(8,128)S(1)}, u32[]{:S(2)}, u32[]{:S(2)}) collective-permute-start(f32[512,128]{0,1:T(8,128)} %get-tuple-element.1014), channel_id=1, source_target_pairs={{0,2},{2,4},{4,6},{6,8},{8,10},{10,12},{12,14},{14,16},{16,18},{18... | collective-permute-start | bytes 786440 | tf_op jit(solution)/shard_map/while/body/eval_jaxpr/ppermute | solution.py:15
  664.2 15.0 %collective-permute-start = (f32[512,128]{0,1:T(8,128)}, f32[512,128]{0,1:T(8,128)S(1)}, u32[]{:S(2)}, u32[]{:S(2)}) collective-permute-start(f32[512,128]{0,1:T(8,128)} %get-tuple-element.1014), channel_id=1, source_target_pairs={{0,2},{2,4},{4,6},{6,8},{8,10},{10,12},{12,14},{14,16},{16,18},{18... | collective-permute-start | bytes 786440 | tf_op jit(solution)/shard_map/while/body/eval_jaxpr/ppermute | solution.py:15
  (38 other events, 54.1 us)
Sparse Core Ops, SparseCore 0:
  18.6 53.6 all-reduce.3
where the time goes:
time: 689 us; the launch traced here: 687 us
  waiting for transfers between devices  501 us (73%)
  starting transfers between devices  87.2 us (13%)
  local copies, waits for them, and re-layouts  53.8 us (8%)
  matrix products  23 us (3%)
  between operations  13.5 us (2%)
  other arithmetic  7.53 us (1%)
    ppermute x34, waiting for transfers between devices, passed_along(): lax.ppermute(value, axis, [(source, source + steps) for source in range(l...  448 us
    ppermute x34, starting transfers between devices, passed_along(): lax.ppermute(value, axis, [(source, source + steps) for source in range(l...  87.2 us
    psum x1, waiting for transfers between devices, per_device(): lax.psum(gram_blocks(genotypes, rim_cols, group), 'smp') / sample_total  53.8 us
    another operation x37, local copies, waits for them, and re-layouts  25.2 us
    while x64, local copies, waits for them, and re-layouts  22.5 us
  transfers between devices with their start and end apart: 35, of which 35 were waited for; matrix products, arithmetic and copies ran while one was open for 0% of the time, Pallas kernels for 0%

commit v1 on v0

v1 whole, which is shorter than its diff:
```python
import functools

import jax
import jax.numpy as jnp
from jax import lax
from jax.experimental import pallas as pl
from jax.experimental.pallas import tpu as pltpu
from jax.sharding import PartitionSpec as P

RIDGE = 0.5
CHUNKS = 2
MESH = pl.DeviceIdType.MESH
F32 = jnp.float32
BF16 = jnp.bfloat16


def halves(x):
    high = x.astype(BF16)
    low = (x - high.astype(F32)).astype(BF16)
    return high, low


def dot(a, b):
    return jnp.dot(a, b, preferred_element_type=F32)


def gram(a, b):
    return lax.dot_general(a, b, (((0,), (0,)), ((), ())), preferred_element_type=F32)


def wide(a, b):
    return dot(a[0], b[0]) + (dot(a[0], b[1]) + dot(a[1], b[0]))


def pair_dot(a, both):
    n = both.shape[1] // 2
    first = dot(a[0], both)
    return first[:, :n] + (first[:, n:] + dot(a[1], both[:, :n]))


def joined(x):
    return jnp.concatenate(halves(x), 1)


def kernel(
    var_count, smp_count, total,
    g_ref, m_ref, b_ref, w_ref,
    mates, rim, u_high, u_low, c_high, c_low, w1_f32, w1_out, w1_in, y_out, y_in, w2_out, w2_in,
    mate_send, mate_recv, rim_send, rim_recv, chain_send, chain_recv,
):
    s = lax.axis_index("var")
    q = lax.axis_index("smp")
    last = var_count - 1
    grp = b_ref.shape[1]
    samples = g_ref.shape[0]
    part = samples // CHUNKS
    right = {"var": s + 1}
    left = {"var": s - 1}
    a_rows, b_rows = pl.ds(0, grp), pl.ds(grp, grp)

    barrier = pltpu.get_barrier_semaphore()

    @pl.when(s > 0)
    def _():
        pl.semaphore_signal(barrier, inc=1, device_id=left, device_id_type=MESH)

    @pl.when(s < last)
    def _():
        pl.semaphore_signal(barrier, inc=1, device_id=right, device_id_type=MESH)

    for k in range(1, smp_count):
        pl.semaphore_signal(
            barrier, inc=1, device_id={"smp": lax.rem(q + k, smp_count)}, device_id_type=MESH
        )
    inner = jnp.logical_and(s > 0, s < last)

    @pl.when(inner)
    def _():
        pl.semaphore_wait(barrier, smp_count + 1)

    @pl.when(jnp.logical_not(inner))
    def _():
        pl.semaphore_wait(barrier, smp_count)

    def mate_copy(k, c):
        rows = pl.ds(c * part, part)
        return pltpu.make_async_remote_copy(
            src_ref=g_ref.at[rows],
            dst_ref=mates.at[k - 1, rows],
            send_sem=mate_send.at[k - 1, c],
            recv_sem=mate_recv.at[k - 1, c],
            device_id={"smp": lax.rem(q + k, smp_count)},
            device_id_type=MESH,
        )

    def rim_copy(k, c):
        rows = pl.ds(c * part, part)
        return pltpu.make_async_remote_copy(
            src_ref=g_ref.at[rows] if k == 0 else mates.at[k - 1, rows],
            dst_ref=rim.at[k, rows],
            send_sem=rim_send.at[k, c],
            recv_sem=rim_recv.at[k, c],
            device_id=right,
            device_id_type=MESH,
        )

    def chain_copy(index, src, dst, target):
        return pltpu.make_async_remote_copy(
            src_ref=src,
            dst_ref=dst,
            send_sem=chain_send.at[index],
            recv_sem=chain_recv.at[index],
            device_id=target,
            device_id_type=MESH,
        )

    w1_copy = chain_copy(0, w1_out, w1_in, right)
    y_copy = chain_copy(1, y_out, y_in, left)
    w2_copy = chain_copy(2, w2_out, w2_in, right)

    for c in range(CHUNKS):
        for k in range(1, smp_count):
            mate_copy(k, c).start()

    @pl.when(s < last)
    def _():
        for c in range(CHUNKS):
            rim_copy(0, c).start()

    inverse = [halves(b_ref[0]), halves(b_ref[1])]
    for c in range(CHUNKS):
        for k in range(1, smp_count):
            mate_copy(k, c).wait_recv()

            @pl.when(s < last)
            def _():
                rim_copy(k, c).start()

    def own_block(i, j):
        ci, cj = pl.ds(i * grp, grp), pl.ds(j * grp, grp)
        acc = gram(g_ref[:, ci], g_ref[:, cj])
        for k in range(1, smp_count):
            acc = acc + gram(mates[k - 1, :, ci], mates[k - 1, :, cj])
        return acc * (1.0 / total)

    a_aa = halves(own_block(0, 0))
    a_bb = halves(own_block(1, 1))
    lower_f32 = own_block(1, 0)
    a_ba = halves(lower_f32)
    a_ab = halves(lower_f32.T)
    s21_f32 = -wide(inverse[1], halves(wide(a_ba, inverse[0])))
    s21 = halves(s21_f32)
    v_a = wide(inverse[0], halves(m_ref[a_rows]))
    v_b = wide(inverse[1], halves(m_ref[b_rows] - wide(a_ba, halves(v_a))))

    @pl.when(s == 0)
    def _():
        w1_f32[a_rows] = v_a
        w1_f32[b_rows] = v_b
        w1_out[a_rows] = joined(v_a)
        w1_out[b_rows] = joined(v_b)

    @pl.when(s > 0)
    def _():
        for c in range(CHUNKS):
            for k in range(smp_count):
                rim_copy(k, c).wait_recv()

        def cross_block(i, j):
            ci, cj = pl.ds(i * grp, grp), pl.ds(j * grp, grp)
            acc = gram(g_ref[:, ci], rim[0, :, cj])
            for k in range(1, smp_count):
                acc = acc + gram(mates[k - 1, :, ci], rim[k, :, cj])
            return acc * (1.0 / total)

        row = lax.broadcasted_iota(jnp.int32, (grp, grp), 0)
        col = lax.broadcasted_iota(jnp.int32, (grp, grp), 1)
        within = col >= row
        a0 = jnp.where(within, cross_block(0, 0), 0.0)
        a1 = cross_block(0, 1)
        b1 = jnp.where(within, cross_block(1, 1), 0.0)
        for n, block in enumerate((a0, a1, b1)):
            high, low = halves(block.T)
            c_high[n] = high
            c_low[n] = low
        a0, a1, b1 = halves(a0), halves(a1), halves(b1)

        def put(rows, cols, value):
            high, low = halves(-value)
            u_high[rows, cols] = high
            u_low[rows, cols] = low

        put(a_rows, a_rows, wide(inverse[0], a0))
        put(a_rows, b_rows, wide(inverse[0], a1))
        put(b_rows, a_rows, wide(s21, a0))
        put(b_rows, b_rows, wide(s21, a1) + wide(inverse[1], b1))

        w1_copy.wait_recv()
        step = pair_dot((u_high[...], u_low[...]), w1_in[...])
        w1_a = v_a + step[:grp]
        w1_b = v_b + step[grp:]
        w1_f32[a_rows] = w1_a
        w1_f32[b_rows] = w1_b
        w1_out[a_rows] = joined(w1_a)
        w1_out[b_rows] = joined(w1_b)

    @pl.when(s < last)
    def _():
        w1_copy.start()

    @pl.when(s > 0)
    def _():
        own_a, own_b = w1_out[a_rows], w1_out[b_rows]
        y_out[a_rows] = joined(pair_dot((c_high[0], c_low[0]), own_a))
        y_out[b_rows] = joined(
            pair_dot((c_high[1], c_low[1]), own_a) + pair_dot((c_high[2], c_low[2]), own_b)
        )
        y_copy.start()

    w1_a, w1_b = w1_f32[a_rows], w1_f32[b_rows]
    pair_a, pair_b = w1_out[a_rows], w1_out[b_rows]
    r_a = m_ref[a_rows] - RIDGE * w1_a - pair_dot(a_aa, pair_a) - pair_dot(a_ab, pair_b)
    h_a = w1_a + pair_dot(inverse[0], joined(r_a))
    r_b = m_ref[b_rows] - RIDGE * w1_b - pair_dot(a_bb, pair_b) - pair_dot(a_ba, joined(h_a))
    h_b = w1_b + pair_dot(inverse[1], joined(r_b))
    w_ref[a_rows] = h_a
    w_ref[b_rows] = h_b

    @pl.when(s < last)
    def _():
        y_copy.wait_recv()
        y_a, y_b = y_in[a_rows], y_in[b_rows]
        w_ref[a_rows] -= pair_dot(inverse[0], y_a)
        w_ref[b_rows] -= pair_dot(s21, y_a) + pair_dot(inverse[1], y_b)

    @pl.when(s > 0)
    def _():
        w2_copy.wait_recv()
        w_ref[...] += pair_dot((u_high[...], u_low[...]), w2_in[...])

    @pl.when(s < last)
    def _():
        w2_out[...] = joined(w_ref[...])
        w2_copy.start()

    for c in range(CHUNKS):
        for k in range(1, smp_count):
            mate_copy(k, c).wait_send()

    @pl.when(s < last)
    def _():
        for c in range(CHUNKS):
            for k in range(smp_count):
                rim_copy(k, c).wait_send()
        w1_copy.wait_send()
        w2_copy.wait_send()

    @pl.when(s > 0)
    def _():
        y_copy.wait_send()


def solution(mesh):
    var_count, smp_count = mesh.shape["var"], mesh.shape["smp"]

    def per_device(genotypes, marginal, block_inverse):
        samples, variants = genotypes.shape
        traits = marginal.shape[1]
        grp = block_inverse.shape[1]
        pair = (variants, 2 * traits)
        mates = max(1, smp_count - 1)
        dma = pltpu.SemaphoreType.DMA
        return pl.pallas_call(
            functools.partial(kernel, var_count, smp_count, samples * smp_count),
            out_shape=jax.ShapeDtypeStruct(marginal.shape, F32),
            in_specs=[pl.BlockSpec(memory_space=pltpu.VMEM)] * 3,
            out_specs=pl.BlockSpec(memory_space=pltpu.VMEM),
            scratch_shapes=[
                pltpu.VMEM((mates, samples, variants), BF16),
                pltpu.VMEM((smp_count, samples, variants), BF16),
                pltpu.VMEM((variants, variants), BF16),
                pltpu.VMEM((variants, variants), BF16),
                pltpu.VMEM((3, grp, grp), BF16),
                pltpu.VMEM((3, grp, grp), BF16),
                pltpu.VMEM((variants, traits), F32),
                pltpu.VMEM(pair, BF16),
                pltpu.VMEM(pair, BF16),
                pltpu.VMEM(pair, BF16),
                pltpu.VMEM(pair, BF16),
                pltpu.VMEM(pair, BF16),
                pltpu.VMEM(pair, BF16),
                dma((mates, CHUNKS)),
                dma((mates, CHUNKS)),
                dma((smp_count, CHUNKS)),
                dma((smp_count, CHUNKS)),
                dma((3,)),
                dma((3,)),
            ],
            compiler_params=pltpu.CompilerParams(
                collective_id=0, has_side_effects=True, vmem_limit_bytes=48 * 1024 * 1024
            ),
        )(genotypes, marginal, block_inverse)

    return jax.shard_map(
        per_device,
        mesh=mesh,
        in_specs=(P("smp", "var"), P("var", "smp"), P("var", None, None)),
        out_specs=P("var", "smp"),
        check_vma=False,
    )
```

time: 689 us -> 90.2 us (0.13)
  waiting for transfers between devices: 501 us -> 0 us
  starting transfers between devices: 87.2 us -> 0 us
  Pallas kernels: 0 us -> 85 us
  local copies, waits for them, and re-layouts: 53.8 us -> 3.74 us
  matrix products: 23 us -> 0 us
  between operations: 13.5 us -> 0.01 us
  other arithmetic: 7.53 us -> 0 us
    ppermute x34 -> x0, waiting for transfers between devices: 448 us -> none  [passed_along(): lax.ppermute(value, axis, [(source, source + steps) for source in range(l...]
    ppermute x34 -> x0, starting transfers between devices: 87.2 us -> none  [passed_along(): lax.ppermute(value, axis, [(source, source + steps) for source in range(l...]
    pallas_call x0 -> x1, Pallas kernels: none -> 85 us  [per_device(): pl.pallas_call(functools.partial(kernel, var_count, smp_count, samples *...]
    psum x1 -> x0, waiting for transfers between devices: 53.8 us -> none  [per_device(): lax.psum(gram_blocks(genotypes, rim_cols, group), 'smp') / sample_total]
    another operation x37 -> x0, local copies, waits for them, and re-layouts: 25.2 us -> none
    dot_general x33 -> x0, matrix products: 23 us -> none  [the longest x8 12.4 us: slab_advance(): jnp.dot(lowered[group_index + 2 - offset, offset].T, lax.dynamic_slice_in...]
    while x65 -> x0, local copies, waits for them, and re-layouts: 22.6 us -> none
  transfers between devices with their start and end apart: 35 -> 0, of which waited for: 35 -> 0; matrix products, arithmetic and copies ran while one was open for 0% -> 0% of each run, Pallas kernels for 0% -> 0%
where the time goes in v1:
time: 90.2 us; the launch traced here: 88.7 us
  Pallas kernels  85 us (94%)
  local copies, waits for them, and re-layouts  3.74 us (4%)
    pallas_call x1, Pallas kernels, per_device(): pl.pallas_call(functools.partial(kernel, var_count, smp_count, samples *...  85 us
    unnamed x7, local copies, waits for them, and re-layouts  3.74 us

profile of v1, /device:TPU:26, one launch (start us, length us, event | category | flops | bytes accessed | tf_op | source)
XLA Modules:
  0.0 88.7 jit_solution(10194822032378921544)
XLA Ops:
  0.0 0.0 copy-start
  0.0 1.0 %copy-done = bf16[512,512]{1,0:T(8,128)(2,1)S(1)} copy-done((bf16[512,512]{1,0:T(8,128)(2,1)S(1)}, bf16[512,512]{1,0:T(8,128)(2,1)}, u32[]{:S(2)}) %copy-start) | copy-done | bytes 524312
  1.0 0.0 copy-start.1
  1.0 1.0 %copy-done.1 = f32[2,256,256]{2,1,0:T(8,128)S(1)} copy-done((f32[2,256,256]{2,1,0:T(8,128)S(1)}, f32[2,256,256]{2,1,0:T(8,128)}, u32[]{:S(2)}) %copy-start.1) | copy-done | bytes 524312
  2.1 0.0 copy-start.2
  2.1 0.9 %copy-done.2 = f32[512,128]{1,0:T(8,128)S(1)} copy-done((f32[512,128]{1,0:T(8,128)S(1)}, f32[512,128]{1,0:T(8,128)}, u32[]{:S(2)}) %copy-start.2) | copy-done | bytes 262168
  3.0 85.0 %shard_map.37 = f32[512,128]{1,0:T(8,128)S(1)} custom-call(bf16[512,512]{1,0:T(8,128)(2,1)S(1)} %copy-done, f32[512,128]{1,0:T(8,128)S(1)} %copy-done.2, f32[2,256,256]{2,1,0:T(8,128)S(1)} %copy-done.1), custom_call_target="tpu_custom_call" | custom-call | tf_op jit(solution)/shard_map/pallas_call | solution.py:273
  88.0 0.7 copy.5
Async XLA Ops:
  0.0 1.0 %copy-start = (bf16[512,512]{1,0:T(8,128)(2,1)S(1)}, bf16[512,512]{1,0:T(8,128)(2,1)}, u32[]{:S(2)}) copy-start(bf16[512,512]{1,0:T(8,128)(2,1)} %g_ref.1) | copy-start | bytes 1572868
  1.0 1.0 %copy-start.1 = (f32[2,256,256]{2,1,0:T(8,128)S(1)}, f32[2,256,256]{2,1,0:T(8,128)}, u32[]{:S(2)}) copy-start(f32[2,256,256]{2,1,0:T(8,128)} %b_ref.1) | copy-start | bytes 1572868
  2.1 0.9 %copy-start.2 = (f32[512,128]{1,0:T(8,128)S(1)}, f32[512,128]{1,0:T(8,128)}, u32[]{:S(2)}) copy-start(f32[512,128]{1,0:T(8,128)} %m_ref.1) | copy-start | bytes 786436

commit v2 on v1

v2 whole, which is shorter than its diff:
```python
import functools

import jax
import jax.numpy as jnp
from jax import lax
from jax.experimental import pallas as pl
from jax.experimental.pallas import tpu as pltpu
from jax.sharding import PartitionSpec as P

RIDGE = 0.5
CHUNKS = 4
PARTS = 2
MESH = pl.DeviceIdType.MESH
F32 = jnp.float32
BF16 = jnp.bfloat16


def halves(x):
    high = x.astype(BF16)
    low = (x - high.astype(F32)).astype(BF16)
    return high, low


def dot(a, b):
    return jnp.dot(a, b, preferred_element_type=F32)


def gram(a, b):
    return lax.dot_general(a, b, (((0,), (0,)), ((), ())), preferred_element_type=F32)


def wide(a, b):
    return dot(a[0], b[0]) + (dot(a[0], b[1]) + dot(a[1], b[0]))


def pair_dot(a, both):
    n = both.shape[1] // 2
    first = dot(a[0], both)
    return first[:, :n] + (first[:, n:] + dot(a[1], both[:, :n]))


def joined(x):
    return jnp.concatenate(halves(x), 1)


def kernel(
    var_count, smp_count, total,
    g_hbm, m_hbm, b_hbm, w_hbm,
    g_ref, m_ref, b_ref, w_ref,
    mates, rim, cross, u_high, u_low, in_high, in_low, chip_high, chip_low, c_high, c_low,
    v_f32, v_out, v_in, w1_f32, h_f32, w1_out, x1_in, x1_pass, y_out, y_in, h_out, h_in,
    w2_out, x2_in, x2_pass,
    local_sem, mate_send, mate_recv, rim_send, rim_recv, u_send, u_recv, chain_send, chain_recv,
):
    s = lax.axis_index("var")
    q = lax.axis_index("smp")
    last = var_count - 1
    grp = b_ref.shape[1]
    samples = g_ref.shape[0]
    piece = samples // CHUNKS
    wide_part = m_ref.shape[1] // PARTS
    even = lax.rem(s, 2) == 0
    odd = jnp.logical_not(even)
    right, left = {"var": s + 1}, {"var": s - 1}
    next_chip = {"var": s + 2}
    a_rows, b_rows = pl.ds(0, grp), pl.ds(grp, grp)
    both = jnp.logical_and

    locals_ = [
        pltpu.make_async_copy(g_hbm, g_ref, local_sem.at[0]),
        pltpu.make_async_copy(m_hbm, m_ref, local_sem.at[1]),
        pltpu.make_async_copy(b_hbm, b_ref, local_sem.at[2]),
    ]
    for copy in locals_:
        copy.start()

    barrier = pltpu.get_barrier_semaphore()

    def greet(target):
        pl.semaphore_signal(barrier, inc=1, device_id=target, device_id_type=MESH)

    for k in range(1, smp_count):
        greet({"smp": lax.rem(q + k, smp_count)})
    pl.when(s > 0)(lambda: greet(left))
    pl.when(s < last)(lambda: greet(right))
    pl.when(both(odd, s > 1))(lambda: greet({"var": s - 2}))
    pl.when(both(odd, s < last))(lambda: greet(next_chip))
    mate_count = smp_count - 1

    def gather(count):
        return lambda: pl.semaphore_wait(barrier, mate_count + count)

    pl.when(s == 0)(gather(1))
    pl.when(both(even, s > 0))(gather(2))
    pl.when(s == 1)(gather(3))
    pl.when(both(odd, both(s > 1, s < last)))(gather(4))
    pl.when(s == last)(gather(2))

    def remote(src, dst, send, recv, target):
        return pltpu.make_async_remote_copy(
            src_ref=src, dst_ref=dst, send_sem=send, recv_sem=recv,
            device_id=target, device_id_type=MESH,
        )

    def mate_copy(k, c):
        rows = pl.ds(c * piece, piece)
        return remote(
            g_hbm.at[rows], mates.at[k - 1, rows],
            mate_send.at[k - 1, c], mate_recv.at[k - 1, c],
            {"smp": lax.rem(q + k, smp_count)},
        )

    def rim_copy(k, c):
        rows = pl.ds(c * piece, piece)
        return remote(
            g_hbm.at[rows] if k == 0 else mates.at[k - 1, rows], rim.at[k, rows],
            rim_send.at[k, c], rim_recv.at[k, c], right,
        )

    def chain_copy(kind, h, src, dst, target):
        return remote(src.at[h], dst.at[h], chain_send.at[kind, h], chain_recv.at[kind, h], target)

    def x1_copy(h):
        return chain_copy(0, h, w1_out, x1_in, next_chip)

    def x1_on(h):
        return chain_copy(1, h, x1_in, x1_pass, left)

    def y_copy(h):
        return chain_copy(2, h, y_out, y_in, left)

    def h_copy(h):
        return chain_copy(3, h, h_out, h_in, right)

    def x2_copy(h):
        return chain_copy(4, h, w2_out, x2_in, next_chip)

    def x2_on(h):
        return chain_copy(5, h, x2_in, x2_pass, left)

    def v_copy(h):
        return chain_copy(6, h, v_out, v_in, right)

    u_copies = [
        remote(u_high, in_high, u_send.at[0], u_recv.at[0], right),
        remote(u_low, in_low, u_send.at[1], u_recv.at[1], right),
    ]

    for c in range(CHUNKS):
        for k in range(1, smp_count):
            mate_copy(k, c).start()

    @pl.when(s < last)
    def _():
        for c in range(CHUNKS):
            rim_copy(0, c).start()

    for copy in locals_:
        copy.wait()

    def own_grams(ref):
        a, b = ref[:, a_rows], ref[:, b_rows]
        return [gram(a, a), gram(b, b), gram(b, a)]

    def cross_grams(ref, other):
        a, b = ref[:, a_rows], ref[:, b_rows]
        return [gram(a, other[:, a_rows]), gram(a, other[:, b_rows]), gram(b, other[:, b_rows])]

    def take(c):
        for k in range(1, smp_count):
            mate_copy(k, c).wait_recv()

            @pl.when(s < last)
            def _():
                rim_copy(k, c).start()

    inverse = [halves(b_ref[0]), halves(b_ref[1])]
    own = own_grams(g_ref)
    for c in range(CHUNKS // 2):
        take(c)

    @pl.when(s > 0)
    def _():
        for c in range(CHUNKS):
            rim_copy(0, c).wait_recv()
        for n, block in enumerate(cross_grams(g_ref, rim.at[0])):
            cross[n] = block

    for c in range(CHUNKS // 2, CHUNKS):
        take(c)
    for k in range(1, smp_count):
        own = [x + y for x, y in zip(own, own_grams(mates.at[k - 1]))]
    own = [x * (1.0 / total) for x in own]
    a_aa, a_bb, a_ba = halves(own[0]), halves(own[1]), halves(own[2])
    a_ab = halves(own[2].T)
    s21 = halves(-wide(inverse[1], halves(wide(a_ba, inverse[0]))))
    v_a = wide(inverse[0], halves(m_ref[a_rows]))
    v_b = wide(inverse[1], halves(m_ref[b_rows] - wide(a_ba, halves(v_a))))

    for h in range(PARTS):
        cols = slice(h * wide_part, (h + 1) * wide_part)
        for rows, value in ((a_rows, v_a), (b_rows, v_b)):
            v_f32[h, rows] = value[:, cols]
            v_out[h, rows] = joined(value[:, cols])

    @pl.when(even)
    def _():
        for h in range(PARTS):
            v_copy(h).start()

    @pl.when(s > 0)
    def _():
        for c in range(CHUNKS):
            for k in range(1, smp_count):
                rim_copy(k, c).wait_recv()
        blocks = [cross[n] for n in range(3)]
        for k in range(1, smp_count):
            blocks = [x + y for x, y in zip(blocks, cross_grams(mates.at[k - 1], rim.at[k]))]
        row = lax.broadcasted_iota(jnp.int32, (grp, grp), 0)
        col = lax.broadcasted_iota(jnp.int32, (grp, grp), 1)
        within = col >= row
        a0, a1, b1 = [x * (1.0 / total) for x in blocks]
        a0, b1 = jnp.where(within, a0, 0.0), jnp.where(within, b1, 0.0)
        for n, block in enumerate((a0, a1, b1)):
            cross[n] = block
        a0, a1, b1 = halves(a0), halves(a1), halves(b1)

        def put(rows, cols, value):
            high, low = halves(-value)
            u_high[rows, cols] = high
            u_low[rows, cols] = low

        put(a_rows, a_rows, wide(inverse[0], a0))
        put(a_rows, b_rows, wide(inverse[0], a1))
        put(b_rows, a_rows, wide(s21, a0))
        put(b_rows, b_rows, wide(s21, a1) + wide(inverse[1], b1))

        @pl.when(even)
        def _():
            for copy in u_copies:
                copy.start()

        for n in range(3):
            high, low = halves(cross[n].T)
            c_high[n] = high
            c_low[n] = low

    def send_y(h):
        own_a, own_b = w1_out[h, a_rows], w1_out[h, b_rows]
        y_out[h, a_rows] = joined(pair_dot((c_high[0], c_low[0]), own_a))
        y_out[h, b_rows] = joined(
            pair_dot((c_high[1], c_low[1]), own_a) + pair_dot((c_high[2], c_low[2]), own_b)
        )
        y_copy(h).start()

    def u():
        return u_high[...], u_low[...]

    def chip():
        return chip_high[...], chip_low[...]

    @pl.when(odd)
    def _():
        @pl.when(s > 1)
        def _():
            for copy in u_copies:
                copy.wait_recv()
            high, low = halves(wide(u(), (in_high[...], in_low[...])))
            chip_high[...] = high
            chip_low[...] = low

        for h in range(PARTS):
            v_copy(h).wait_recv()
            v_f32[h] += pair_dot(u(), v_in[h])

    for h in range(PARTS):
        @pl.when(s < 2)
        def _():
            w1_f32[h] = v_f32[h]
            w1_out[h] = joined(v_f32[h])

        @pl.when(both(even, s > 0))
        def _():
            x1_on(h).wait_recv()
            value = v_f32[h] + pair_dot(u(), x1_pass[h])
            w1_f32[h] = value
            w1_out[h] = joined(value)

        @pl.when(both(odd, s > 1))
        def _():
            x1_copy(h).wait_recv()
            x1_on(h).start()
            value = v_f32[h] + pair_dot(chip(), x1_in[h])
            w1_f32[h] = value
            w1_out[h] = joined(value)

        @pl.when(both(odd, s < last))
        def _():
            x1_copy(h).start()

        @pl.when(both(even, s > 0))
        def _():
            send_y(h)

    @pl.when(odd)
    def _():
        for h in range(PARTS):
            send_y(h)

    for h in range(PARTS):
        cols = slice(h * wide_part, (h + 1) * wide_part)
        w1_a, w1_b = w1_f32[h, a_rows], w1_f32[h, b_rows]
        pair_a, pair_b = w1_out[h, a_rows], w1_out[h, b_rows]
        m_a, m_b = m_ref[a_rows][:, cols], m_ref[b_rows][:, cols]
        r_a = m_a - RIDGE * w1_a - pair_dot(a_aa, pair_a) - pair_dot(a_ab, pair_b)
        h_a = w1_a + pair_dot(inverse[0], joined(r_a))
        r_b = m_b - RIDGE * w1_b - pair_dot(a_bb, pair_b) - pair_dot(a_ba, joined(h_a))
        h_f32[h, a_rows] = h_a
        h_f32[h, b_rows] = w1_b + pair_dot(inverse[1], joined(r_b))

    for h in range(PARTS):
        @pl.when(s < last)
        def _():
            y_copy(h).wait_recv()
            y_a, y_b = y_in[h, a_rows], y_in[h, b_rows]
            h_f32[h, a_rows] -= pair_dot(inverse[0], y_a)
            h_f32[h, b_rows] -= pair_dot(s21, y_a) + pair_dot(inverse[1], y_b)

        @pl.when(even)
        def _():
            h_out[h] = joined(h_f32[h])
            h_copy(h).start()

    for h in range(PARTS):
        @pl.when(odd)
        def _():
            h_copy(h).wait_recv()
            h_f32[h] += pair_dot(u(), h_in[h])

    for h in range(PARTS):
        @pl.when(both(even, s > 0))
        def _():
            x2_on(h).wait_recv()
            if_even = h_f32[h] + pair_dot(u(), x2_pass[h])
            h_f32[h] = if_even

        @pl.when(both(odd, s > 1))
        def _():
            x2_copy(h).wait_recv()
            x2_on(h).start()
            h_f32[h] += pair_dot(chip(), x2_in[h])

        @pl.when(both(odd, s < last))
        def _():
            w2_out[h] = joined(h_f32[h])
            x2_copy(h).start()

    w_ref[...] = jnp.concatenate([h_f32[h] for h in range(PARTS)], 1)
    out = pltpu.make_async_copy(w_ref, w_hbm, local_sem.at[0])
    out.start()
    out.wait()

    for c in range(CHUNKS):
        for k in range(1, smp_count):
            mate_copy(k, c).wait_send()

    @pl.when(s < last)
    def _():
        for c in range(CHUNKS):
            for k in range(smp_count):
                rim_copy(k, c).wait_send()

    def sent(*copies):
        def wait():
            for copy in copies:
                for h in range(PARTS):
                    copy(h).wait_send()
        return wait

    pl.when(s > 0)(sent(y_copy))
    pl.when(even)(sent(v_copy, h_copy))
    pl.when(both(odd, s < last))(sent(x1_copy, x2_copy))
    pl.when(both(odd, s > 1))(sent(x1_on, x2_on))

    @pl.when(both(even, s > 0))
    def _():
        for copy in u_copies:
            copy.wait_send()


def solution(mesh):
    var_count, smp_count = mesh.shape["var"], mesh.shape["smp"]

    def per_device(genotypes, marginal, block_inverse):
        samples, variants = genotypes.shape
        traits = marginal.shape[1]
        grp = block_inverse.shape[1]
        part_f32 = pltpu.VMEM((PARTS, variants, traits // PARTS), F32)
        pair = pltpu.VMEM((PARTS, variants, 2 * traits // PARTS), BF16)
        square = pltpu.VMEM((variants, variants), BF16)
        mates = max(1, smp_count - 1)
        dma = pltpu.SemaphoreType.DMA
        return pl.pallas_call(
            functools.partial(kernel, var_count, smp_count, samples * smp_count),
            out_shape=jax.ShapeDtypeStruct(marginal.shape, F32),
            in_specs=[pl.BlockSpec(memory_space=pltpu.HBM)] * 3,
            out_specs=pl.BlockSpec(memory_space=pltpu.HBM),
            scratch_shapes=[
                pltpu.VMEM((samples, variants), BF16),
                pltpu.VMEM((variants, traits), F32),
                pltpu.VMEM(block_inverse.shape, F32),
                pltpu.VMEM((variants, traits), F32),
                pltpu.VMEM((mates, samples, variants), BF16),
                pltpu.VMEM((smp_count, samples, variants), BF16),
                pltpu.VMEM((3, grp, grp), F32),
            ]
            + [square] * 6
            + [pltpu.VMEM((3, grp, grp), BF16)] * 2
            + [part_f32, pair, pair, part_f32, part_f32]
            + [pair] * 10
            + [
                dma((3,)),
                dma((mates, CHUNKS)),
                dma((mates, CHUNKS)),
                dma((smp_count, CHUNKS)),
                dma((smp_count, CHUNKS)),
                dma((2,)),
                dma((2,)),
                dma((7, PARTS)),
                dma((7, PARTS)),
            ],
            compiler_params=pltpu.CompilerParams(
                collective_id=0, has_side_effects=True, vmem_limit_bytes=48 * 1024 * 1024
            ),
        )(genotypes, marginal, block_inverse)

    return jax.shard_map(
        per_device,
        mesh=mesh,
        in_specs=(P("smp", "var"), P("var", "smp"), P("var", None, None)),
        out_specs=P("var", "smp"),
        check_vma=False,
    )
```

time: 90.2 us -> 66.6 us (0.74); the launches traced: 88.7 us -> 66.4 us
  Pallas kernels: 85 us -> 62.7 us
    pallas_call x1, Pallas kernels: 85 us -> 62.7 us  [per_device(): pl.pallas_call(functools.partial(kernel, var_count, smp_count, samples *...]
where the time goes in v2:
time: 66.6 us; the launch traced here: 66.4 us
  Pallas kernels  62.7 us (94%)
  local copies, waits for them, and re-layouts  3.74 us (6%)
    pallas_call x1, Pallas kernels, per_device(): pl.pallas_call(functools.partial(kernel, var_count, smp_count, samples *...  62.7 us
    unnamed x7, local copies, waits for them, and re-layouts  3.74 us

profile of v2, /device:TPU:26, one launch (start us, length us, event | category | flops | bytes accessed | tf_op | source)
XLA Modules:
  0.0 66.4 jit_solution(12377825008466220976)
XLA Ops:
  0.0 0.0 copy-start
  0.0 1.0 %copy-done = bf16[512,512]{1,0:T(8,128)(2,1)S(1)} copy-done((bf16[512,512]{1,0:T(8,128)(2,1)S(1)}, bf16[512,512]{1,0:T(8,128)(2,1)}, u32[]{:S(2)}) %copy-start) | copy-done | bytes 524312
  1.0 0.0 copy-start.1
  1.0 1.0 %copy-done.1 = f32[2,256,256]{2,1,0:T(8,128)S(1)} copy-done((f32[2,256,256]{2,1,0:T(8,128)S(1)}, f32[2,256,256]{2,1,0:T(8,128)}, u32[]{:S(2)}) %copy-start.1) | copy-done | bytes 524312
  2.1 0.0 copy-start.2
  2.1 0.9 %copy-done.2 = f32[512,128]{1,0:T(8,128)S(1)} copy-done((f32[512,128]{1,0:T(8,128)S(1)}, f32[512,128]{1,0:T(8,128)}, u32[]{:S(2)}) %copy-start.2) | copy-done | bytes 262168
  3.0 62.7 %shard_map.37 = f32[512,128]{1,0:T(8,128)S(1)} custom-call(bf16[512,512]{1,0:T(8,128)(2,1)S(1)} %copy-done, f32[512,128]{1,0:T(8,128)S(1)} %copy-done.2, f32[2,256,256]{2,1,0:T(8,128)S(1)} %copy-done.1), custom_call_target="tpu_custom_call" | custom-call | tf_op jit(solution)/shard_map/pallas_call | solution.py:403
  65.7 0.7 %copy.5 = f32[512,128]{1,0:T(8,128)} copy(f32[512,128]{1,0:T(8,128)S(1)} %shard_map.37) | data formatting | bytes 524288
Async XLA Ops:
  0.0 1.0 %copy-start = (bf16[512,512]{1,0:T(8,128)(2,1)S(1)}, bf16[512,512]{1,0:T(8,128)(2,1)}, u32[]{:S(2)}) copy-start(bf16[512,512]{1,0:T(8,128)(2,1)} %g_hbm.1) | copy-start | bytes 1572868
  1.0 1.0 %copy-start.1 = (f32[2,256,256]{2,1,0:T(8,128)S(1)}, f32[2,256,256]{2,1,0:T(8,128)}, u32[]{:S(2)}) copy-start(f32[2,256,256]{2,1,0:T(8,128)} %b_hbm.1) | copy-start | bytes 1572868
  2.1 0.9 %copy-start.2 = (f32[512,128]{1,0:T(8,128)S(1)}, f32[512,128]{1,0:T(8,128)}, u32[]{:S(2)}) copy-start(f32[512,128]{1,0:T(8,128)} %m_hbm.1) | copy-start | bytes 786436

commit v3 on v2

--- a/solution.py
+++ b/solution.py
@@ -45,11 +45,12 @@
 
 def kernel(
     var_count, smp_count, total,
-    g_hbm, m_hbm, b_hbm, w_hbm,
-    g_ref, m_ref, b_ref, w_ref,
-    mates, rim, cross, u_high, u_low, in_high, in_low, chip_high, chip_low, c_high, c_low,
+    g_hbm, m_hbm, b_hbm, w_ref,
+    g_ref, m_ref, b_ref,
+    mates, rim, cross, u_high, u_low, in_high, in_low, chip_high, chip_low,
+    map_high, map_low, far_high, far_low, c_high, c_low,
     v_f32, v_out, v_in, w1_f32, h_f32, w1_out, x1_in, x1_pass, y_out, y_in, h_out, h_in,
-    w2_out, x2_in, x2_pass,
+    w2_out, x2_in, x2_pass, c0_out, c0_in, far_out, far_in,
     local_sem, mate_send, mate_recv, rim_send, rim_recv, u_send, u_recv, chain_send, chain_recv,
 ):
     s = lax.axis_index("var")
@@ -146,6 +147,17 @@
         remote(u_low, in_low, u_send.at[1], u_recv.at[1], right),
     ]
 
+    def c0_copy(h):
+        return chain_copy(7, h, c0_out, c0_in, right)
+
+    def far_copy(h):
+        return chain_copy(8, h, far_out, far_in, {"var": s - 2})
+
+    map_copies = [
+        remote(map_high, far_high, u_send.at[2], u_recv.at[2], right),
+        remote(map_low, far_low, u_send.at[3], u_recv.at[3], right),
+    ]
+
     for c in range(CHUNKS):
         for k in range(1, smp_count):
             mate_copy(k, c).start()
@@ -207,6 +219,13 @@
     def _():
         for h in range(PARTS):
             v_copy(h).start()
+
+    def couple(ref, h, out):
+        own_a, own_b = ref[h, a_rows], ref[h, b_rows]
+        out[h, a_rows] = joined(pair_dot((c_high[0], c_low[0]), own_a))
+        out[h, b_rows] = joined(
+            pair_dot((c_high[1], c_low[1]), own_a) + pair_dot((c_high[2], c_low[2]), own_b)
+        )
 
     @pl.when(s > 0)
     def _():
@@ -245,13 +264,22 @@
             c_high[n] = high
             c_low[n] = low
 
-    def send_y(h):
-        own_a, own_b = w1_out[h, a_rows], w1_out[h, b_rows]
-        y_out[h, a_rows] = joined(pair_dot((c_high[0], c_low[0]), own_a))
-        y_out[h, b_rows] = joined(
-            pair_dot((c_high[1], c_low[1]), own_a) + pair_dot((c_high[2], c_low[2]), own_b)
-        )
-        y_copy(h).start()
+        @pl.when(even)
+        def _():
+            top = u_high[a_rows], u_low[a_rows]
+            low_rows = u_high[b_rows], u_low[b_rows]
+            c = [(c_high[n], c_low[n]) for n in range(3)]
+            high, low = halves(wide(c[0], top))
+            map_high[a_rows] = high
+            map_low[a_rows] = low
+            high, low = halves(wide(c[1], top) + wide(c[2], low_rows))
+            map_high[b_rows] = high
+            map_low[b_rows] = low
+            for copy in map_copies:
+                copy.start()
+            for h in range(PARTS):
+                couple(v_out, h, c0_out)
+                c0_copy(h).start()
 
     def u():
         return u_high[...], u_low[...]
@@ -261,6 +289,10 @@
 
     @pl.when(odd)
     def _():
+        for h in range(PARTS):
+            v_copy(h).wait_recv()
+            v_f32[h] += pair_dot(u(), v_in[h])
+
         @pl.when(s > 1)
         def _():
             for copy in u_copies:
@@ -268,10 +300,10 @@
             high, low = halves(wide(u(), (in_high[...], in_low[...])))
             chip_high[...] = high
             chip_low[...] = low
-
-        for h in range(PARTS):
-            v_copy(h).wait_recv()
-            v_f32[h] += pair_dot(u(), v_in[h])
+            for copy in map_copies:
+                copy.wait_recv()
+            for h in range(PARTS):
+                c0_copy(h).wait_recv()
 
     for h in range(PARTS):
         @pl.when(s < 2)
@@ -298,14 +330,18 @@
         def _():
             x1_copy(h).start()
 
-        @pl.when(both(even, s > 0))
-        def _():
-            send_y(h)
+        @pl.when(both(odd, s > 1))
+        def _():
+            sent_by = (c0_in[h].astype(F32), far_high[...], far_low[...])
+            start = sent_by[0][:, :wide_part] + sent_by[0][:, wide_part:]
+            far_out[h] = joined(start + pair_dot(sent_by[1:], x1_in[h]))
+            far_copy(h).start()
 
     @pl.when(odd)
     def _():
         for h in range(PARTS):
-            send_y(h)
+            couple(w1_out, h, y_out)
+            y_copy(h).start()
 
     for h in range(PARTS):
         cols = slice(h * wide_part, (h + 1) * wide_part)
@@ -318,13 +354,21 @@
         h_f32[h, a_rows] = h_a
         h_f32[h, b_rows] = w1_b + pair_dot(inverse[1], joined(r_b))
 
-    for h in range(PARTS):
-        @pl.when(s < last)
+    def couple_back(h, ref):
+        y_a, y_b = ref[h, a_rows], ref[h, b_rows]
+        h_f32[h, a_rows] -= pair_dot(inverse[0], y_a)
+        h_f32[h, b_rows] -= pair_dot(s21, y_a) + pair_dot(inverse[1], y_b)
+
+    for h in range(PARTS):
+        @pl.when(both(odd, s < last))
+        def _():
+            far_copy(h).wait_recv()
+            couple_back(h, far_in)
+
+        @pl.when(even)
         def _():
             y_copy(h).wait_recv()
-            y_a, y_b = y_in[h, a_rows], y_in[h, b_rows]
-            h_f32[h, a_rows] -= pair_dot(inverse[0], y_a)
-            h_f32[h, b_rows] -= pair_dot(s21, y_a) + pair_dot(inverse[1], y_b)
+            couple_back(h, y_in)
 
         @pl.when(even)
         def _():
@@ -356,10 +400,6 @@
             x2_copy(h).start()
 
     w_ref[...] = jnp.concatenate([h_f32[h] for h in range(PARTS)], 1)
-    out = pltpu.make_async_copy(w_ref, w_hbm, local_sem.at[0])
-    out.start()
-    out.wait()
-
     for c in range(CHUNKS):
         for k in range(1, smp_count):
             mate_copy(k, c).wait_send()
@@ -377,14 +417,15 @@
                     copy(h).wait_send()
         return wait
 
-    pl.when(s > 0)(sent(y_copy))
+    pl.when(odd)(sent(y_copy))
     pl.when(even)(sent(v_copy, h_copy))
     pl.when(both(odd, s < last))(sent(x1_copy, x2_copy))
-    pl.when(both(odd, s > 1))(sent(x1_on, x2_on))
+    pl.when(both(odd, s > 1))(sent(x1_on, x2_on, far_copy))
+    pl.when(both(even, s > 0))(sent(c0_copy))
 
     @pl.when(both(even, s > 0))
     def _():
-        for copy in u_copies:
+        for copy in u_copies + map_copies:
             copy.wait_send()
 
 
@@ -404,33 +445,32 @@
             functools.partial(kernel, var_count, smp_count, samples * smp_count),
             out_shape=jax.ShapeDtypeStruct(marginal.shape, F32),
             in_specs=[pl.BlockSpec(memory_space=pltpu.HBM)] * 3,
-            out_specs=pl.BlockSpec(memory_space=pltpu.HBM),
+            out_specs=pl.BlockSpec(memory_space=pltpu.VMEM),
             scratch_shapes=[
                 pltpu.VMEM((samples, variants), BF16),
                 pltpu.VMEM((variants, traits), F32),
                 pltpu.VMEM(block_inverse.shape, F32),
-                pltpu.VMEM((variants, traits), F32),
                 pltpu.VMEM((mates, samples, variants), BF16),
                 pltpu.VMEM((smp_count, samples, variants), BF16),
                 pltpu.VMEM((3, grp, grp), F32),
             ]
-            + [square] * 6
+            + [square] * 10
             + [pltpu.VMEM((3, grp, grp), BF16)] * 2
             + [part_f32, pair, pair, part_f32, part_f32]
-            + [pair] * 10
+            + [pair] * 14
             + [
                 dma((3,)),
                 dma((mates, CHUNKS)),
                 dma((mates, CHUNKS)),
                 dma((smp_count, CHUNKS)),
                 dma((smp_count, CHUNKS)),
-                dma((2,)),
-                dma((2,)),
-                dma((7, PARTS)),
-                dma((7, PARTS)),
+                dma((4,)),
+                dma((4,)),
+                dma((9, PARTS)),
+                dma((9, PARTS)),
             ],
             compiler_params=pltpu.CompilerParams(
-                collective_id=0, has_side_effects=True, vmem_limit_bytes=48 * 1024 * 1024
+                collective_id=0, has_side_effects=True, vmem_limit_bytes=(64 * 1024 - 96) * 1024
             ),
         )(genotypes, marginal, block_inverse)
 

time: 66.6 us -> 63.5 us (0.953)
  local copies, waits for them, and re-layouts: 3.74 us -> 1.67 us
  Pallas kernels: 62.7 us -> 61.7 us
    unnamed x7 -> x1, local copies, waits for them, and re-layouts: 3.74 us -> 1.67 us
    pallas_call x1, Pallas kernels: 62.7 us -> 61.7 us  [per_device(): pl.pallas_call(functools.partial(kernel, var_count, smp_count, samples *...]
where the time goes in v3:
time: 63.5 us; the launch traced here: 63.4 us
  Pallas kernels  61.7 us (97%)
  local copies, waits for them, and re-layouts  1.67 us (3%)
    pallas_call x1, Pallas kernels, per_device(): pl.pallas_call(functools.partial(kernel, var_count, smp_count, samples *...  61.7 us
    unnamed x1, local copies, waits for them, and re-layouts  1.67 us

profile of v3, /device:TPU:26, one launch (start us, length us, event | category | flops | bytes accessed | tf_op | source)
XLA Modules:
  0.0 63.4 jit_solution(13881222801155942772)
XLA Ops:
  0.0 61.7 %shard_map.37 = f32[512,128]{1,0:T(8,128)} custom-call(bf16[512,512]{1,0:T(8,128)(2,1)} %g_hbm.1, f32[512,128]{1,0:T(8,128)} %m_hbm.1, f32[2,256,256]{2,1,0:T(8,128)} %b_hbm.1), custom_call_target="tpu_custom_call" | custom-call | tf_op jit(solution)/shard_map/pallas_call | solution.py:444
  61.7 1.7 %copy.5 = f32[512,128]{1,0:T(8,128)} copy(f32[512,128]{1,0:T(8,128)} %shard_map.37) | data formatting | bytes 524288

commit v4 on v3

--- a/solution.py
+++ b/solution.py
@@ -266,6 +266,9 @@
 
         @pl.when(even)
         def _():
+            for h in range(PARTS):
+                couple(v_out, h, c0_out)
+                c0_copy(h).start()
             top = u_high[a_rows], u_low[a_rows]
             low_rows = u_high[b_rows], u_low[b_rows]
             c = [(c_high[n], c_low[n]) for n in range(3)]
@@ -277,9 +280,6 @@
             map_low[b_rows] = low
             for copy in map_copies:
                 copy.start()
-            for h in range(PARTS):
-                couple(v_out, h, c0_out)
-                c0_copy(h).start()
 
     def u():
         return u_high[...], u_low[...]
@@ -300,10 +300,6 @@
             high, low = halves(wide(u(), (in_high[...], in_low[...])))
             chip_high[...] = high
             chip_low[...] = low
-            for copy in map_copies:
-                copy.wait_recv()
-            for h in range(PARTS):
-                c0_copy(h).wait_recv()
 
     for h in range(PARTS):
         @pl.when(s < 2)
@@ -332,6 +328,10 @@
 
         @pl.when(both(odd, s > 1))
         def _():
+            if h == 0:
+                for copy in map_copies:
+                    copy.wait_recv()
+            c0_copy(h).wait_recv()
             sent_by = (c0_in[h].astype(F32), far_high[...], far_low[...])
             start = sent_by[0][:, :wide_part] + sent_by[0][:, wide_part:]
             far_out[h] = joined(start + pair_dot(sent_by[1:], x1_in[h]))
@@ -360,28 +360,25 @@
         h_f32[h, b_rows] -= pair_dot(s21, y_a) + pair_dot(inverse[1], y_b)
 
     for h in range(PARTS):
+        @pl.when(even)
+        def _():
+            y_copy(h).wait_recv()
+            couple_back(h, y_in)
+            h_out[h] = joined(h_f32[h])
+            h_copy(h).start()
+
+    for h in range(PARTS):
+        @pl.when(odd)
+        def _():
+            h_copy(h).wait_recv()
+            h_f32[h] += pair_dot(u(), h_in[h])
+
+    for h in range(PARTS):
         @pl.when(both(odd, s < last))
         def _():
             far_copy(h).wait_recv()
             couple_back(h, far_in)
 
-        @pl.when(even)
-        def _():
-            y_copy(h).wait_recv()
-            couple_back(h, y_in)
-
-        @pl.when(even)
-        def _():
-            h_out[h] = joined(h_f32[h])
-            h_copy(h).start()
-
-    for h in range(PARTS):
-        @pl.when(odd)
-        def _():
-            h_copy(h).wait_recv()
-            h_f32[h] += pair_dot(u(), h_in[h])
-
-    for h in range(PARTS):
         @pl.when(both(even, s > 0))
         def _():
             x2_on(h).wait_recv()

time: 63.5 us -> 62.7 us (0.987)
  Pallas kernels: 61.7 us -> 60.9 us
    pallas_call x1, Pallas kernels: 61.7 us -> 60.9 us  [per_device(): pl.pallas_call(functools.partial(kernel, var_count, smp_count, samples *...]
where the time goes in v4:
time: 62.7 us; the launch traced here: 62.6 us
  Pallas kernels  60.9 us (97%)
  local copies, waits for them, and re-layouts  1.67 us (3%)
    pallas_call x1, Pallas kernels, per_device(): pl.pallas_call(functools.partial(kernel, var_count, smp_count, samples *...  60.9 us
    unnamed x1, local copies, waits for them, and re-layouts  1.67 us

profile of v4, /device:TPU:26, one launch (start us, length us, event | category | flops | bytes accessed | tf_op | source)
XLA Modules:
  0.0 62.6 jit_solution(17182939727080593225)
XLA Ops:
  0.0 60.9 %shard_map.37 = f32[512,128]{1,0:T(8,128)} custom-call(bf16[512,512]{1,0:T(8,128)(2,1)} %g_hbm.1, f32[512,128]{1,0:T(8,128)} %m_hbm.1, f32[2,256,256]{2,1,0:T(8,128)} %b_hbm.1), custom_call_target="tpu_custom_call" | custom-call | tf_op jit(solution)/shard_map/pallas_call | solution.py:441
  60.9 1.7 %copy.5 = f32[512,128]{1,0:T(8,128)} copy(f32[512,128]{1,0:T(8,128)} %shard_map.37) | data formatting | bytes 524288

commit v5 on v4

--- a/solution.py
+++ b/solution.py
@@ -8,7 +8,7 @@
 from jax.sharding import PartitionSpec as P
 
 RIDGE = 0.5
-CHUNKS = 4
+CHUNKS = 8
 PARTS = 2
 MESH = pl.DeviceIdType.MESH
 F32 = jnp.float32

time: 62.7 us -> 62.4 us (level)
  no operation moved by 1% of the time
where the time goes in v5:
time: 62.4 us; the launch traced here: 62.3 us
  Pallas kernels  60.6 us (97%)
  local copies, waits for them, and re-layouts  1.67 us (3%)
    pallas_call x1, Pallas kernels, per_device(): pl.pallas_call(functools.partial(kernel, var_count, smp_count, samples *...  60.6 us
    unnamed x1, local copies, waits for them, and re-layouts  1.67 us

profile of v5, /device:TPU:26, one launch (start us, length us, event | category | flops | bytes accessed | tf_op | source)
XLA Modules:
  0.0 62.3 jit_solution(6288787723895170126)
XLA Ops:
  0.0 60.6 %shard_map.37 = f32[512,128]{1,0:T(8,128)} custom-call(bf16[512,512]{1,0:T(8,128)(2,1)} %g_hbm.1, f32[512,128]{1,0:T(8,128)} %m_hbm.1, f32[2,256,256]{2,1,0:T(8,128)} %b_hbm.1), custom_call_target="tpu_custom_call" | custom-call | tf_op jit(solution)/shard_map/pallas_call | solution.py:441
  60.6 1.7 %copy.5 = f32[512,128]{1,0:T(8,128)} copy(f32[512,128]{1,0:T(8,128)} %shard_map.37) | data formatting | bytes 524288
